TPU v7x, 128 devices: a whole 4x4x4 slice. The times are simulated.
128 devices in a mesh: row: 16 (over y, x_lo, core), col: 8 (over x_hi, z).
Axes of the slice: x: 4 (x_hi: 2, x_lo: 2; x = x_hi * 2 + x_lo), y: 4, z: 4, core: 2. Of those that a mesh axis runs over, the one named last changes fastest.
Arguments:
- features: bfloat16 [65536, 256], P(('row', 'col')), may hold values from -6 to 6
- weight: bfloat16 [256, 256], replicated, may hold values from -0.375 to 0.375
- bias: float32 [256], replicated, may hold values from -3 to 3
- tile_values: bfloat16 [16, 8, 448, 128, 128], P('row', 'col'), may hold values from -0.09375 to 0.09375
- tile_index: int32 [16, 8, 448, 2], P('row', 'col'), may hold values from 0 to 63, as said below
- tile_count: int32 [16, 8], P('row', 'col'), may hold values from 1 to 448
- out_grad: bfloat16 [65536, 256], P(('row', 'col')), may hold values from -6 to 6
Outputs:
- output: bfloat16 [65536, 256], P(('row', 'col'))
- feat_grad: bfloat16 [65536, 256], P(('row', 'col'))
- weight_grad: float32 [256, 256], replicated
- bias_grad: float32 [256], replicated
Inputs may be any that keep to these rules, and one draw needn't show every extreme that they name: `tile_index`: column k is a row tile (below 32) for k = 0 and a column tile for k = 1; the slots of one cell name distinct tile positions.
All inputs are finite; a program needn't handle non-finite values.
Results may differ from a plain program's by a relative error of at most 0.007.
Values may be sent and summed in bfloat16 or wider, within the bound.
A program may use at most 128 MiB of HBM per device.

v0:
```python
import jax
import jax.numpy as jnp
from jax import lax
from jax.sharding import PartitionSpec as P


def spread(values, target, source_idx, live, count, source, target_tiles, flip):
    width = source.shape[1]
    tile = values.shape[1]
    slots = values.shape[0]
    blocks = source.reshape(-1, tile, width)
    step = min(64, slots)
    turns = (count + step - 1) // step

    def one(number, acc):
        start = number * step
        vals = lax.dynamic_slice_in_dim(values, start, step, 0)
        dest = lax.dynamic_slice_in_dim(target, start, step, 0)
        anchor = lax.dynamic_slice_in_dim(source_idx, start, step, 0)
        alive = lax.dynamic_slice_in_dim(live, start, step, 0)
        picked = blocks[anchor]
        if flip:
            product = jnp.einsum("tab,taf->tbf", vals, picked, preferred_element_type=jnp.float32)
        else:
            product = jnp.einsum("tab,tbf->taf", vals, picked, preferred_element_type=jnp.float32)
        product = jnp.where(alive[:, None, None], product, jnp.zeros_like(product))
        return acc.at[dest].add(product)

    start_acc = jnp.zeros((target_tiles, tile, width), jnp.float32)
    acc = lax.fori_loop(0, turns, one, start_acc)
    return acc.reshape(target_tiles * tile, width)


def shards(features, weight, bias, tile_values, tile_index, tile_count, out_grad):
    values = tile_values[0, 0]
    index = tile_index[0, 0]
    count = tile_count[0, 0]
    tile = values.shape[1]
    owned = features.shape[0]
    live = jnp.arange(values.shape[0], dtype=jnp.int32) < count
    row_tiles = owned * lax.axis_size("col") // tile
    col_tiles = owned * lax.axis_size("row") // tile
    projected = jnp.dot(features, weight, preferred_element_type=jnp.float32).astype(jnp.bfloat16)
    column = lax.all_gather(projected, "row", axis=0, tiled=True)
    partial_value = spread(values, index[:, 0], index[:, 1], live, count, column, row_tiles, False)
    pre = lax.psum_scatter(partial_value, "col", scatter_dimension=0, tiled=True) + bias
    sig = jax.nn.sigmoid(pre)
    output = (pre * sig).astype(jnp.bfloat16)
    slope = sig * (1.0 + pre * (1.0 - sig))
    pre_grad = (out_grad.astype(jnp.float32) * slope).astype(jnp.bfloat16)
    grad_rows = lax.all_gather(pre_grad, "col", axis=0, tiled=True)
    back_partial = spread(values, index[:, 1], index[:, 0], live, count, grad_rows, col_tiles, True)
    back = lax.psum_scatter(back_partial, "row", scatter_dimension=0, tiled=True).astype(
        jnp.bfloat16
    )
    feat_grad = jnp.dot(back, weight.T, preferred_element_type=jnp.float32).astype(jnp.bfloat16)
    local_weight = jnp.dot(features.T, back, preferred_element_type=jnp.float32)
    local_bias = jnp.sum(pre_grad.astype(jnp.float32), axis=0)
    weight_grad, bias_grad = lax.psum((local_weight, local_bias), ("row", "col"))
    return (output, feat_grad, weight_grad, bias_grad)


def solution(mesh):
    return jax.shard_map(
        shards,
        mesh=mesh,
        in_specs=(
            P(("row", "col"), None),
            P(),
            P(),
            P("row", "col", None, None, None),
            P("row", "col", None, None),
            P("row", "col"),
            P(("row", "col"), None),
        ),
        out_specs=(P(("row", "col"), None), P(("row", "col"), None), P(), P()),
        check_vma=False,
    )
```

profile of v0, /device:TPU:1, one launch (start us, length us, event | category | flops | bytes accessed | tf_op | source)
XLA Modules:
  0.0 874.3 jit_solution(6959296506524315647)
XLA Ops:
  7.2 0.9 copy-done
  8.1 1.8 convolution_convert_fusion.1
  10.0 0.0 reduce-scatter.3.cloned.1.call-start
  10.7 0.8 fusion.6
  11.5 39.8 %all-gather.3.cloned.1.call-done = bf16[8192,256]{1,0:T(8,128)(2,1)} async-done(((bf16[512,256]{1,0:T(8,128)(2,1)}), bf16[8192,256]{1,0:T(8,128)(2,1)}) %all-gather.3.cloned.1.call-update) | async-done | bytes 4194320 | tf_op jit(solution)/shard_map/all_gather | solution.py:44
  51.3 2.4 broadcast_in_dim.31
  53.7 31.6 %while.20 = (s32[]{:T(128)}, f32[32,128,256]{2,1,0:T(8,128)}, s32[]{:T(128)}, s32[448]{0:T(512)S(1)}, pred[448]{0:T(512)(128)(4,1)S(1)}, /*index=5*/bf16[448,128...) while((s32[]{:T(128)}, f32[32,128,256]{2,1,0:T(8,128)}, ...), condition=%wide.region_2.3_spmd, body=%wide.region_0.2_spmd.sunk | while | flops 541066624 | bytes 48240752 | solution.py:30
  53.7 0.1 dynamic_slice.40
  53.8 0.1 compare_select_fusion.6
  53.9 4.9 gather_fusion
  58.8 7.3 broadcast_select_fusion.4
  66.1 19.2 %scatter_fusion = f32[32,128,256]{2,1,0:T(8,128)} fusion(f32[32,128,256]{2,1,0:T(8,128)} %get-tuple-element.266, s32[64]{0:T(128)S(1)} %get-tuple-element.241, f32[64,128,256]{2,1,0:T(8,128)} %broadcast_select_fusion.4), kind=kCustom, calls=%fused_computation.2.clone.1 | custom fusion | flops 2097152 | bytes 25166080 | tf_op jit(solution)/shard_map/while/body/scatter-add | solution.py:27
  85.3 0.0 all-gather.5.cloned.1.call-start
  85.4 269.2 %reduce-scatter.3.cloned.1.call-done = f32[512,256]{1,0:T(8,128)} async-done(((f32[4096,256]{1,0:T(8,128)}), f32[512,256]{1,0:T(8,128)}) %reduce-scatter.3.cloned.1.call-update) | async-done | bytes 524304 | tf_op jit(solution)/shard_map/reduce_scatter | solution.py:46
  354.6 2.1 convert_reduce_fusion
  356.7 0.0 reduce-scatter.5.cloned.1.call-start
  356.7 19.9 %copy.11 = bf16[1,1,448,128,128]{3,4,2,1,0:T(8,128)(2,1)} copy(bf16[1,1,448,128,128]{4,3,2,1,0:T(8,128)(2,1)} %bitcast.29) | data formatting | bytes 29360128 | tf_op args[3]
  376.6 34.7 %all-gather.5.cloned.1.call-done = bf16[4096,256]{1,0:T(8,128)(2,1)} async-done(((bf16[512,256]{1,0:T(8,128)(2,1)}), bf16[4096,256]{1,0:T(8,128)(2,1)}) %all-gather.5.cloned.1.call-update) | async-done | bytes 2097168 | tf_op jit(solution)/shard_map/all_gather | solution.py:51
  411.3 4.4 broadcast.35
  415.7 29.8 %while.21 = (s32[]{:T(128)}, f32[64,128,256]{2,1,0:T(8,128)}, s32[]{:T(128)}, s32[448]{0:T(512)S(1)}, pred[448]{0:T(512)(128)(4,1)S(1)}, /*index=5*/bf16[448,128...) while((s32[]{:T(128)}, f32[64,128,256]{2,1,0:T(8,128)}, ...), condition=%wide.region_6.7_spmd, body=%wide.region_4.6_spmd.sunk | while | flops 541066624 | bytes 48240752 | solution.py:30
  415.7 0.1 dynamic_slice.43
  415.8 0.1 compare_select_fusion.7
  415.8 2.8 gather_fusion.1
  418.6 7.3 broadcast_select_fusion.5
  426.0 19.5 %scatter_fusion.1 = f32[64,128,256]{2,1,0:T(8,128)} fusion(f32[64,128,256]{2,1,0:T(8,128)} %get-tuple-element.302, s32[64]{0:T(128)S(1)} %get-tuple-element.251, f32[64,128,256]{2,1,0:T(8,128)} %broadcast_select_fusion.5), kind=kCustom, calls=%fused_computation.3.clone.1 | custom fusion | flops 2097152 | bytes 25166080 | tf_op jit(solution)/shard_map/while/body/scatter-add | solution.py:27
  445.5 0.0 all-reduce.2.cloned.1.call-start
  445.6 242.0 %psum.15 = f32[256]{0:T(256)} all-reduce(f32[256]{0:T(256)S(1)} %get-tuple-element.136), channel_id=1, replica_groups=mesh['row'=16,'col'=8] {'row','col'}, use_global_device_ids=true, to_apply=%region_10.11 | all-reduce | flops 256 | bytes 2048 | tf_op jit(solution)/shard_map/psum | solution.py:59
  687.5 30.5 %reduce-scatter.5.cloned.1.call-done = f32[512,256]{1,0:T(8,128)} async-done(((f32[8192,256]{1,0:T(8,128)}), f32[512,256]{1,0:T(8,128)}) %reduce-scatter.5.cloned.1.call-update) | async-done | bytes 524304 | tf_op jit(solution)/shard_map/reduce_scatter | solution.py:53
  718.0 2.0 convolution_bitcast_fusion
  720.0 2.0 convolution_convert_fusion
  722.0 143.9 %all-reduce.2.cloned.1.call-done = f32[256,256]{0,1:T(8,128)} async-done(((f32[256,256]{0,1:T(8,128)}), f32[256,256]{0,1:T(8,128)}) %all-reduce.2.cloned.1.call-update) | async-done | bytes 262160 | tf_op jit(solution)/shard_map/psum | solution.py:59
  866.0 1.8 copy.13
  (18 shorter events, 0.2 us)
Async XLA Ops:
  7.2 1.0 copy-start
  7.2 44.1 %all-gather.3.cloned.1.call-start = ((), (), s32[]{:S(2)}) async-start(), calls=%async_computation.2 | async-start | bytes 4456448 | tf_op jit(solution)/shard_map/all_gather | solution.py:44
  10.0 344.6 %reduce-scatter.3.cloned.1.call-start = ((), (), s32[]{:S(2)}) async-start(), calls=%async_computation.3 | async-start | bytes 4718592 | tf_op jit(solution)/shard_map/reduce_scatter | solution.py:46
  85.3 269.2 %copy-start.3 = (bf16[512,256]{1,0:T(8,128)(2,1)S(1)}, bf16[512,256]{1,0:T(8,128)(2,1)}, u32[]{:S(2)}) copy-start(bf16[512,256]{1,0:T(8,128)(2,1)} %param.17) | copy-start | bytes 786436
  85.3 269.2 %copy-start.4 = (f32[256]{0:T(256)S(1)}, f32[256]{0:T(256)}, u32[]{:S(2)}) copy-start(f32[256]{0:T(256)} %param.13) | copy-start | bytes 3076
  85.3 326.0 %all-gather.5.cloned.1.call-start = ((), (), s32[]{:S(2)}) async-start(), calls=%async_computation.4 | async-start | bytes 2359296 | tf_op jit(solution)/shard_map/all_gather | solution.py:51
  356.7 361.3 %reduce-scatter.5.cloned.1.call-start = ((), (), s32[]{:S(2)}) async-start(), calls=%async_computation.5 | async-start | bytes 8912896 | tf_op jit(solution)/shard_map/reduce_scatter | solution.py:53
  411.3 4.4 copy-start.1
  445.5 274.5 %copy-start.2 = (bf16[256,256]{1,0:T(8,128)(2,1)S(1)}, bf16[256,256]{1,0:T(8,128)(2,1)}, u32[]{:S(2)}) copy-start(bf16[256,256]{1,0:T(8,128)(2,1)} %param.12) | copy-start | bytes 393220
  445.5 420.5 %all-reduce.2.cloned.1.call-start = ((), (), s32[]{:S(2)}) async-start(), calls=%async_computation.6 | async-start | bytes 524288 | tf_op jit(solution)/shard_map/psum | solution.py:59
Sparse Core Ops, SparseCore 0:
  10.3 40.9 all-gather.2
  85.5 269.0 reduce-scatter.2
  357.8 53.5 all-gather.4
  445.6 272.3 reduce-scatter.4
  723.9 142.0 all-reduce.1
where the time goes:
time: 876 us; the launch traced here: 874 us
  waiting for transfers between devices  518 us (59%)
  blocking collectives  242 us (28%)
  other arithmetic  41 us (5%)
  local copies, waits for them, and re-layouts  38.1 us (4%)
  matrix products  20.5 us (2%)
  between operations  14.5 us (2%)
    reduce_scatter x1, waiting for transfers between devices, shards(): lax.psum_scatter(partial_value, 'col', scatter_dimension=0, tiled=True)  269 us
    psum x1, blocking collectives, shards(): lax.psum((local_weight, local_bias), ('row', 'col'))  242 us
    psum x1, waiting for transfers between devices, shards(): lax.psum((local_weight, local_bias), ('row', 'col'))  144 us
    all_gather x1, waiting for transfers between devices, shards(): column = lax.all_gather(projected, 'row', axis=0, tiled=True)  39.8 us
    scatter-add x2, other arithmetic, one(): return acc.at[dest].add(product)  38.7 us
    all_gather x1, waiting for transfers between devices, shards(): grad_rows = lax.all_gather(pre_grad, 'col', axis=0, tiled=True)  34.7 us
    reduce_scatter x1, waiting for transfers between devices, shards(): lax.psum_scatter(back_partial, 'row', scatter_dimension=0, tiled=True)  30.5 us
    unnamed x12, local copies, waits for them, and re-layouts  22.6 us
  transfers between devices with their start and end apart: 5, of which 5 were waited for; matrix products, arithmetic and copies ran while one was open for 3% of the time, Pallas kernels for 0%

commit v1 on v0

v1 whole, which is shorter than its diff:
```python
import functools

import jax
import jax.numpy as jnp
from jax import lax
from jax.experimental import pallas as pl
from jax.experimental.pallas import tpu as pltpu
from jax.sharding import PartitionSpec as P

MESH = pl.DeviceIdType.MESH
TILE = 128
BLK = 4
SLOTS = 448
NR, NC = 32, 64
FPAIRS, BPAIRS = 240, 256
ZERO_RUN = 256
UNROLL = 4
F32, BF16, I32 = jnp.float32, jnp.bfloat16, jnp.int32


def pair_lists(dst_r, dst_c, src_c, live_r, live_c, nd, ns):
    t_r = lax.broadcasted_iota(I32, (SLOTS, SLOTS), 1)
    t_c = lax.broadcasted_iota(I32, (SLOTS, SLOTS), 0)
    one = lambda m: m.astype(I32)
    dlive_r = jnp.where(live_r, dst_r, nd)
    dlive_c = jnp.where(live_c, dst_c, nd)
    own_cn = dlive_c == lax.broadcasted_iota(I32, (SLOTS, nd), 1)
    own_nr = dlive_r == lax.broadcasted_iota(I32, (nd, SLOTS), 0)
    n_r = jnp.sum(one(own_cn), axis=0, keepdims=True)
    n_c = jnp.sum(one(own_nr), axis=1, keepdims=True)
    half_c = (n_c + 1) // 2
    half_r = (n_r + 1) // 2
    g_c = lax.broadcasted_iota(I32, (nd, nd), 0)
    g_r = lax.broadcasted_iota(I32, (nd, nd), 1)
    base_r = jnp.sum(jnp.where(g_c < g_r, half_c, 0), axis=0, keepdims=True)
    base_c = jnp.sum(jnp.where(g_r < g_c, half_r, 0), axis=1, keepdims=True)
    rank_c = jnp.sum(one((dlive_c == dlive_r) & (t_r < t_c)), axis=1, keepdims=True)
    pos_c = jnp.sum(jnp.where(own_cn, 2 * base_r, 0), axis=1, keepdims=True) + rank_c
    pos_c = jnp.where(live_c, pos_c, 4096)
    hit = pos_c == lax.broadcasted_iota(I32, (SLOTS, 512), 1)
    slot = lax.broadcasted_iota(I32, (SLOTS, 512), 0)
    tile_l = jnp.sum(jnp.where(hit, slot, 0), axis=0, keepdims=True)
    src_l = jnp.sum(jnp.where(hit, src_c - ns, 0), axis=0, keepdims=True) + ns
    first = (base_c == lax.broadcasted_iota(I32, (nd, 512), 1)) & (n_c > 0)
    keep_l = 1 - jnp.sum(one(first), axis=0, keepdims=True)
    end_r = jnp.where(n_r > 0, base_r + half_r - 1, ZERO_RUN)
    return tile_l, src_l, keep_l, end_r


def kernel(H, feat, weight, bias, tiles_hbm, idx_c, idx_r, cnt, ograd,
           output, fgrad, dw_out, db_out,
           tiles, runs, lists_v, lists, xs, ps, gs, qs, sib, rsa, rsb, rsa2, rsb2, sa, sb, ybf, zb,
           dbuf, drs, dp, dq, dfin, ss, rs, ls):
    w = 256 // H
    i, j = lax.axis_index("row"), lax.axis_index("col")
    y, xl, c = i // 4, lax.rem(i // 2, 2), lax.rem(i, 2)
    xh, z = j // 4, lax.rem(j, 4)
    m4 = lambda v: lax.rem(v + 4, 4)

    class Row:
        p, q = y, xl
        slot = staticmethod(lambda p, q: (p * 2 + q) * 2 + c)
        dev = staticmethod(lambda p, q: ((p * 2 + q) * 2 + c, j))

    class Col:
        p, q = z, xh
        slot = staticmethod(lambda p, q: q * 4 + p)
        dev = staticmethod(lambda p, q: (i, q * 4 + p))

    sibling = ((y * 2 + xl) * 2 + 1 - c, j)
    peers = [lax.rem(i + d, 16) for d in range(1, 16)]
    cpeers = [lax.rem(j + d, 8) for d in range(1, 8)]

    sent = []

    def send(src, dst, dev):
        n = len(sent)
        cp = pltpu.make_async_remote_copy(src_ref=src, dst_ref=dst, send_sem=ss.at[n], recv_sem=rs.at[n],
                                          device_id=dev, device_id_type=MESH)
        cp.start()
        sent.append(cp)
        return cp

    load_tiles = pltpu.make_async_copy(tiles_hbm.at[0, 0], tiles, ls.at[0])
    load_tiles.start()
    loads = []
    for h in range(H):
        for t in range(BLK):
            cp = pltpu.make_async_copy(feat.at[pl.ds(t * TILE, TILE), pl.ds(h * w, w)], xs[h].at[i * BLK + t],
                                       ls.at[1 + h * BLK + t])
            cp.start()
            loads.append(cp)

    barrier = pltpu.get_barrier_semaphore()
    for r in peers:
        pl.semaphore_signal(barrier, inc=1, device_id=(r, j), device_id_type=MESH)
    for k in cpeers:
        pl.semaphore_signal(barrier, inc=1, device_id=(i, k), device_id_type=MESH)
    pl.semaphore_wait(barrier, 22)
    for cp in loads:
        cp.wait()

    blk = lambda buf, s, lo=0, n=BLK: buf.at[pl.ds(s * BLK + lo, n)]

    def gather(g, buf, relay):
        p, q = g.p, g.q
        own = blk(buf, g.slot(p, q))
        down = []
        cx = send(own, own, g.dev(p, 1 - q))
        cy = {d: send(own, own, g.dev(m4(p + d), q)) for d in (1, 3, 2)}
        if relay:
            down.append(send(own, own, sibling))
        yield
        cx.wait_recv()
        s = g.slot(p, 1 - q)
        part = blk(buf, s, 2, 2)
        cb = {d: send(part, part, g.dev(m4(p + d), q)) for d in (1, 3, 2)}
        if relay:
            down.append(send(blk(buf, s), blk(buf, s), sibling))
        ca = {}
        for d in (1, 3, 2):
            cy[d].wait_recv()
            s = g.slot(m4(p - d), q)
            part = blk(buf, s, 0, 2)
            ca[d] = send(part, part, g.dev(p, 1 - q))
            if relay:
                down.append(send(blk(buf, s), blk(buf, s), sibling))
        yield
        for d in (1, 3, 2):
            cb[d].wait_recv()
            ca[d].wait_recv()
            if relay:
                s = g.slot(m4(p - d), 1 - q)
                down.append(send(blk(buf, s), blk(buf, s), sibling))
        for cp in down:
            cp.wait_recv()

    def scatter(g, buf, k, h, emit):
        p, q = g.p, g.q
        ra, rb, ra2, rb2, oa, ob = rsa[k][h], rsb[k][h], rsa2[k][h], rsb2[k][h], sa[k][h], sb[k][h]
        xa, yb = {}, {}
        for d in (1, 3, 2, 0):
            xa[d] = send(blk(buf, g.slot(m4(p + d), 1 - q), 0, 2), ra.at[pl.ds(2 * d, 2)], g.dev(p, 1 - q))
        for d in (1, 3, 2):
            for e in (1, 0):
                qq = 1 - q if e else q
                yb[d, e] = send(blk(buf, g.slot(m4(p + d), qq), 2, 2), rb.at[pl.ds((d - 1) * 4 + e * 2, 2)],
                                g.dev(m4(p + d), q))
        yield
        y2 = {}
        for d in (1, 3, 2):
            xa[d].wait_recv()
            for t in range(2):
                own = buf[g.slot(m4(p + d), q) * BLK + t].astype(F32)
                oa[2 * d + t] = (own + ra[2 * d + t].astype(F32)).astype(BF16)
            y2[d] = send(oa.at[pl.ds(2 * d, 2)], ra2.at[pl.ds(2 * (d - 1), 2)], g.dev(m4(p + d), q))
        for d in (1, 3, 2):
            yb[d, 1].wait_recv()
        for t in range(2):
            tot = buf[g.slot(p, 1 - q) * BLK + 2 + t].astype(F32)
            for d in (1, 3, 2):
                tot = tot + rb[(d - 1) * 4 + 2 + t].astype(F32)
            ob[t] = tot.astype(BF16)
        x2 = send(ob, rb2, g.dev(p, 1 - q))
        yield
        xa[0].wait_recv()
        for d in (1, 3, 2):
            y2[d].wait_recv()
            yb[d, 0].wait_recv()
        for t in range(2):
            tot = buf[g.slot(p, q) * BLK + t].astype(F32) + ra[t].astype(F32)
            for d in (1, 3, 2):
                tot = tot + ra2[2 * (d - 1) + t].astype(F32)
            emit(t, tot)
        x2.wait_recv()
        for t in range(2):
            tot = buf[g.slot(p, q) * BLK + 2 + t].astype(F32)
            for d in (1, 3, 2):
                tot = tot + rb[(d - 1) * 4 + t].astype(F32)
            emit(2 + t, tot + rb2[t].astype(F32))

    def spmm(row, pairs, src, flip):
        dims = (((0,), (0,)), ((), ())) if flip else (((1,), (0,)), ((), ()))

        def body(n, acc):
            for u in range(UNROLL):
                k = n * UNROLL + u
                prod = lax.dot_general(tiles[lists[row, 2 * k]], src[lists[row + 1, 2 * k]], dims,
                                       preferred_element_type=F32)
                prod += lax.dot_general(tiles[lists[row, 2 * k + 1]], src[lists[row + 1, 2 * k + 1]], dims,
                                        preferred_element_type=F32)
                acc = acc * lists[row + 2, k].astype(F32) + prod
                runs[k] = acc.astype(BF16)
            return acc

        lax.fori_loop(0, pairs // UNROLL, body, jnp.zeros((TILE, w), F32))

    def collect(row, nd, dst):
        def body(r, _):
            dst[r] = runs[lists[row + 3, r]]
            return 0

        lax.fori_loop(0, nd, body, 0)

    def finish(gen):
        for _ in gen:
            pass

    ag = [gather(Row, xs[h], True) for h in range(H)]
    for g in ag:
        next(g)

    live_r = lax.broadcasted_iota(I32, (1, SLOTS), 1) < cnt[0, 0]
    live_c = lax.broadcasted_iota(I32, (SLOTS, 1), 0) < cnt[0, 0]
    r_r, c_r = idx_r[0:1, :], idx_r[1:2, :]
    r_c, c_c = idx_c[:, 0:1], idx_c[:, 1:2]
    lists_v[...] = jnp.zeros_like(lists_v)
    for row, (a, b, cc, nd, ns) in ((0, (r_r, r_c, c_c, NR, NC)), (4, (c_r, c_c, r_c, NC, NR))):
        t_l, s_l, k_l, e_l = pair_lists(a, b, cc, live_r, live_c, nd, ns)
        lists_v[row:row + 1, :] = t_l
        lists_v[row + 1:row + 2, :] = s_l
        lists_v[row + 2:row + 3, :] = k_l
        lists_v[row + 3:row + 4, 0:nd] = e_l
    cp = pltpu.make_async_copy(lists_v, lists, ls.at[1 + H * BLK])
    cp.start()
    runs[ZERO_RUN] = jnp.zeros((TILE, w), BF16)
    for h in range(H):
        xs[h][NC] = jnp.zeros((TILE, w), BF16)
        gs[h][NR] = jnp.zeros((TILE, w), BF16)
    cp.wait()
    load_tiles.wait()

    def put_y(h):
        def emit(t, v):
            ybf[pl.ds(t * TILE, TILE), pl.ds(h * w, w)] = v.astype(BF16)
        return emit

    sc = []
    for h in range(H):
        finish(ag[h])
        spmm(0, FPAIRS, xs[h], False)
        collect(0, NR, ps[h])
        g = scatter(Col, ps[h], 0, h, put_y(h))
        next(g)
        sc.append(g)
    for g in sc:
        finish(g)

    wb = weight[...]
    bsum = jnp.zeros((1, 256), F32)
    for t in range(BLK):
        rows = pl.ds(t * TILE, TILE)
        pre = jnp.dot(ybf[rows, :], wb, preferred_element_type=F32) + bias[...]
        sig = 1.0 / (1.0 + jnp.exp(-pre))
        output[rows, :] = (pre * sig).astype(BF16)
        slope = sig * (1.0 + pre * (1.0 - sig))
        pg = (ograd[rows, :].astype(F32) * slope).astype(BF16)
        bsum = bsum + jnp.sum(pg.astype(F32), axis=0, keepdims=True)
        zb[rows, :] = pg
        gw = lax.dot_general(pg, wb, (((1,), (1,)), ((), ())), preferred_element_type=F32).astype(BF16)
        for h in range(H):
            gs[h][j * BLK + t] = gw[:, h * w:(h + 1) * w]
    agc = [gather(Col, gs[h], False) for h in range(H)]
    for g in agc:
        next(g)

    dw = lax.dot_general(ybf[...], zb[...], (((0,), (0,)), ((), ())), preferred_element_type=F32)
    for k in range(8):
        dbuf[k, 0:32, :] = dw[k * 32:(k + 1) * 32, :]
        dbuf[k, 32:40, :] = jnp.broadcast_to(bsum, (8, 256))
    s1 = [send(dbuf.at[lax.rem(j + d, 8)], drs.at[j], (i, lax.rem(j + d, 8))) for d in range(1, 8)]
    drs[j] = dbuf[j]

    for h in range(H):
        next(agc[h])

    for cp in s1:
        cp.wait_recv()
    tot = drs[0]
    for k in range(1, 8):
        tot = tot + drs[k]
    me4 = xl * 2 + c
    dp[me4] = tot
    s2 = []
    for d in range(1, 4):
        o = lax.rem(me4 + d, 4)
        s2.append(send(dp.at[me4], dp.at[me4], (y * 4 + o, j)))

    def grad_2():
        for cp in s2:
            cp.wait_recv()
        dq[y] = (dp[0] + dp[1]) + (dp[2] + dp[3])
        return [send(dq.at[y], dq.at[y], (m4(y + d) * 4 + me4, j)) for d in (1, 3, 2)]

    def grad_3(s3):
        for cp in s3:
            cp.wait_recv()
        dfin[j] = (dq[0] + dq[1]) + (dq[2] + dq[3])
        return [send(dfin.at[j], dfin.at[j], (i, lax.rem(j + d, 8))) for d in range(1, 8)]

    def put_f(h):
        def emit(t, v):
            fgrad[pl.ds(t * TILE, TILE), pl.ds(h * w, w)] = v.astype(BF16)
        return emit

    late = None
    back = []
    for h in range(H):
        finish(agc[h])
        if h == 0:
            s3 = grad_2()
        spmm(4, BPAIRS, gs[h], True)
        collect(4, NC, qs[h])
        if h == 0:
            s4 = grad_3(s3)
        cps = {}
        for k in range(8):
            s = k * 2 + 1 - c
            cps[k] = send(blk(qs[h], s), sib[h].at[pl.ds(k * BLK, BLK)], sibling)
        for k in range(8):
            cps[k].wait_recv()
            for t in range(BLK):
                at = (k * 2 + c) * BLK + t
                qs[h][at] = (qs[h][at].astype(F32) + sib[h][k * BLK + t].astype(F32)).astype(BF16)
        g = scatter(Row, qs[h], 1, h, put_f(h))
        next(g)
        back.append(g)
    for cp in s4:
        cp.wait_recv()
    for k in range(8):
        dw_out[k * 32:(k + 1) * 32, :] = dfin[k, 0:32, :]
    db_out[...] = dfin[0, 32:33, :]
    for g in back:
        finish(g)
    for cp in sent:
        cp.wait_send()


def shards(H, features, weight, bias, tile_values, tile_index, tile_count, out_grad):
    w = 256 // H
    vm = lambda *s, dt=BF16: pltpu.VMEM(s, dt)
    many = lambda n, *s: [vm(n, *s)] * H
    blkT = (TILE, w)
    two = lambda n: [many(n, *blkT) for _ in range(2)]
    index = tile_index[0, 0]
    sems = 180
    scratch = [
        vm(SLOTS, TILE, TILE),
        vm(ZERO_RUN + 1, *blkT),
        vm(8, 512, dt=I32),
        pltpu.SMEM((8, 512), I32),
        many(NC + 1, *blkT),
        many(NR, *blkT),
        many(NR + 1, *blkT),
        many(NC, *blkT),
        many(32, *blkT),
        two(8), two(12), two(6), two(2), two(8), two(2),
        vm(512, 256), vm(512, 256),
        vm(8, 40, 256, dt=F32), vm(8, 40, 256, dt=F32), vm(4, 40, 256, dt=F32), vm(4, 40, 256, dt=F32),
        vm(8, 40, 256, dt=F32),
        pltpu.SemaphoreType.DMA((sems,)), pltpu.SemaphoreType.DMA((sems,)), pltpu.SemaphoreType.DMA((2 + H * BLK,)),
    ]
    vmem = pl.BlockSpec(memory_space=pltpu.VMEM)
    out, fg, dw, db = pl.pallas_call(
        functools.partial(kernel, H),
        out_shape=(
            jax.ShapeDtypeStruct((512, 256), BF16),
            jax.ShapeDtypeStruct((512, 256), BF16),
            jax.ShapeDtypeStruct((256, 256), F32),
            jax.ShapeDtypeStruct((1, 256), F32),
        ),
        in_specs=[pl.BlockSpec(memory_space=pl.ANY), vmem, vmem, pl.BlockSpec(memory_space=pl.ANY), vmem, vmem,
                  pl.BlockSpec(memory_space=pltpu.SMEM), vmem],
        out_specs=(vmem,) * 4,
        scratch_shapes=scratch,
        compiler_params=pltpu.CompilerParams(collective_id=0, has_side_effects=True, vmem_limit_bytes=60 << 20),
        name="layer",
    )(features, weight, bias.reshape(1, 256), tile_values, index, index.T, tile_count, out_grad)
    return out, fg, dw, db.reshape(256)


def solution(mesh):
    return jax.shard_map(
        functools.partial(shards, 1),
        mesh=mesh,
        in_specs=(
            P(("row", "col"), None),
            P(),
            P(),
            P("row", "col", None, None, None),
            P("row", "col", None, None),
            P("row", "col"),
            P(("row", "col"), None),
        ),
        out_specs=(P(("row", "col"), None), P(("row", "col"), None), P(), P()),
        check_vma=False,
    )
```

time: 876 us -> 155 us (0.18)
  waiting for transfers between devices: 518 us -> 0 us
  blocking collectives: 242 us -> 0 us
  Pallas kernels: 0 us -> 146 us
  other arithmetic: 41 us -> 0 us
  local copies, waits for them, and re-layouts: 38.1 us -> 7.75 us
  matrix products: 20.5 us -> 0 us
  between operations: 14.5 us -> 1.29 us
    reduce_scatter x2 -> x0, waiting for transfers between devices: 300 us -> none  [the longest x1 269 us: shards(): lax.psum_scatter(partial_value, 'col', scatter_dimension=0, tiled=True)]
    psum x1 -> x0, blocking collectives: 242 us -> none  [shards(): lax.psum((local_weight, local_bias), ('row', 'col'))]
    pallas_call x0 -> x1, Pallas kernels: none -> 146 us  [shards(): pl.pallas_call(functools.partial(kernel, H), out_shape=(jax.ShapeDtypeStr...]
    psum x1 -> x0, waiting for transfers between devices: 144 us -> none  [shards(): lax.psum((local_weight, local_bias), ('row', 'col'))]
    all_gather x2 -> x0, waiting for transfers between devices: 74.5 us -> none  [the longest x1 39.8 us: shards(): column = lax.all_gather(projected, 'row', axis=0, tiled=True)]
    scatter-add x2 -> x0, other arithmetic: 38.7 us -> none  [one(): return acc.at[dest].add(product)]
    dot_general x5 -> x0, matrix products: 20.5 us -> none  [the longest x1 7.33 us: one(): jnp.einsum('tab,taf->tbf', vals, picked, preferred_element_type=jnp.float32)]
    unnamed x12 -> x4, local copies, waits for them, and re-layouts: 22.6 us -> 6.23 us
  transfers between devices with their start and end apart: 5 -> 0, of which waited for: 5 -> 0; matrix products, arithmetic and copies ran while one was open for 3% -> 0% of each run, Pallas kernels for 0% -> 0%
where the time goes in v1:
time: 155 us
  Pallas kernels  146 us (94%)
  local copies, waits for them, and re-layouts  7.75 us (5%)
    pallas_call x1, Pallas kernels, shards(): pl.pallas_call(functools.partial(kernel, H), out_shape=(jax.ShapeDtypeStr...  146 us
    unnamed x4, local copies, waits for them, and re-layouts  6.23 us

profile of v1, /device:TPU:1, one launch (start us, length us, event | category | flops | bytes accessed | tf_op | source)
XLA Modules:
  0.0 154.6 jit_solution(1401688094262059507)
XLA Ops:
  1.3 1.5 copy.11.idx_c
  2.8 145.6 %layer.1 = (bf16[512,256]{1,0:T(8,128)(2,1)}, bf16[512,256]{1,0:T(8,128)(2,1)}, f32[256,256]{1,0:T(8,128)}, f32[1,256]{1,0:T(1,128)}) custom-call(bf16[512,256]{1,0:T(8,128)(2,1)} %feat.1, bf16[256,256]{1,0:T(8,128)(2,1)} %weight.1, f32[1,256]{1,0:T(1,128)} %bitcast.8, bf16[1,1,448,128,128]{4,3,2,1,0:T(8,128)(2,1)} %tiles_hbm.1, s32[448,2]{1,0:T(8,128)} %copy.11.idx_c, ...), custom_call_target="tpu_custom_call" | custom-call | tf_op jit(solution)/shard_map/layer/pallas_call | solution.py:364
  148.4 1.7 %copy.17 = bf16[512,256]{1,0:T(8,128)(2,1)} copy(bf16[512,256]{1,0:T(8,128)(2,1)} %get-tuple-element.16) | data formatting | bytes 524288
  150.1 1.7 %copy.18 = bf16[512,256]{1,0:T(8,128)(2,1)} copy(bf16[512,256]{1,0:T(8,128)(2,1)} %get-tuple-element.17) | data formatting | bytes 524288
  151.7 1.7 %copy.19 = f32[256,256]{1,0:T(8,128)} copy(f32[256,256]{1,0:T(8,128)} %get-tuple-element.18) | data formatting | bytes 524288
  153.4 1.2 copy.20

commit v2 on v1

--- a/solution.py
+++ b/solution.py
@@ -14,7 +14,7 @@
 NR, NC = 32, 64
 FPAIRS, BPAIRS = 240, 256
 ZERO_RUN = 256
-UNROLL = 4
+FUNROLL, BUNROLL = 24, 32
 F32, BF16, I32 = jnp.float32, jnp.bfloat16, jnp.int32
 
 
@@ -47,9 +47,9 @@
     return tile_l, src_l, keep_l, end_r
 
 
-def kernel(H, feat, weight, bias, tiles_hbm, idx_c, idx_r, cnt, ograd,
-           output, fgrad, dw_out, db_out,
-           tiles, runs, lists_v, lists, xs, ps, gs, qs, sib, rsa, rsb, rsa2, rsb2, sa, sb, ybf, zb,
+def kernel(H, feat, weight, bias, tiles_hbm, idx_r, cnt, ograd_hbm,
+           output_hbm, fgrad_hbm, dw_hbm, db_hbm,
+           ograd, output, fgrad, dw_out, db_out, tiles, runs, lists_v, lists, xs, ps, gs, qs, sib, rsa, rsb, rsa2, rsb2, sa, sb, ybf, zb,
            dbuf, drs, dp, dq, dfin, ss, rs, ls):
     w = 256 // H
     i, j = lax.axis_index("row"), lax.axis_index("col")
@@ -82,7 +82,7 @@
         return cp
 
     load_tiles = pltpu.make_async_copy(tiles_hbm.at[0, 0], tiles, ls.at[0])
-    load_tiles.start()
+    load_grad = pltpu.make_async_copy(ograd_hbm, ograd, ls.at[2 + H * BLK])
     loads = []
     for h in range(H):
         for t in range(BLK):
@@ -91,6 +91,8 @@
             cp.start()
             loads.append(cp)
 
+    load_tiles.start()
+    load_grad.start()
     barrier = pltpu.get_barrier_semaphore()
     for r in peers:
         pl.semaphore_signal(barrier, inc=1, device_id=(r, j), device_id_type=MESH)
@@ -104,34 +106,41 @@
 
     def gather(g, buf, relay):
         p, q = g.p, g.q
-        own = blk(buf, g.slot(p, q))
         down = []
-        cx = send(own, own, g.dev(p, 1 - q))
-        cy = {d: send(own, own, g.dev(m4(p + d), q)) for d in (1, 3, 2)}
-        if relay:
-            down.append(send(own, own, sibling))
+
+        def pass_on(s, lo, n):
+            if relay:
+                part = blk(buf, s, lo, n)
+                down.append(send(part, part, sibling))
+
+        def push(s, lo, n, dev):
+            part = blk(buf, s, lo, n)
+            return send(part, part, dev)
+
+        me = g.slot(p, q)
+        first = {d: push(me, 0, 2, g.dev(m4(p + d), q)) for d in (1, 3, 2)}
+        cx = push(me, 0, BLK, g.dev(p, 1 - q))
+        pass_on(me, 0, BLK)
         yield
         cx.wait_recv()
-        s = g.slot(p, 1 - q)
-        part = blk(buf, s, 2, 2)
-        cb = {d: send(part, part, g.dev(m4(p + d), q)) for d in (1, 3, 2)}
-        if relay:
-            down.append(send(blk(buf, s), blk(buf, s), sibling))
-        ca = {}
-        for d in (1, 3, 2):
-            cy[d].wait_recv()
-            s = g.slot(m4(p - d), q)
-            part = blk(buf, s, 0, 2)
-            ca[d] = send(part, part, g.dev(p, 1 - q))
-            if relay:
-                down.append(send(blk(buf, s), blk(buf, s), sibling))
+        other = g.slot(p, 1 - q)
+        second = {d: push(me, 2, 2, g.dev(m4(p + d), q)) for d in (1, 3, 2)}
+        third = {d: push(other, 2, 2, g.dev(m4(p + d), q)) for d in (1, 3, 2)}
+        pass_on(other, 0, BLK)
+        fourth = {}
+        for d in (1, 3, 2):
+            first[d].wait_recv()
+            fourth[d] = push(g.slot(m4(p - d), q), 0, 2, g.dev(p, 1 - q))
+        for d in (1, 3, 2):
+            pass_on(g.slot(m4(p - d), q), 0, 2)
         yield
         for d in (1, 3, 2):
-            cb[d].wait_recv()
-            ca[d].wait_recv()
-            if relay:
-                s = g.slot(m4(p - d), 1 - q)
-                down.append(send(blk(buf, s), blk(buf, s), sibling))
+            second[d].wait_recv()
+            pass_on(g.slot(m4(p - d), q), 2, 2)
+        for d in (1, 3, 2):
+            third[d].wait_recv()
+            fourth[d].wait_recv()
+            pass_on(g.slot(m4(p - d), 1 - q), 0, BLK)
         for cp in down:
             cp.wait_recv()
 
@@ -179,21 +188,20 @@
                 tot = tot + rb[(d - 1) * 4 + t].astype(F32)
             emit(2 + t, tot + rb2[t].astype(F32))
 
-    def spmm(row, pairs, src, flip):
-        dims = (((0,), (0,)), ((), ())) if flip else (((1,), (0,)), ((), ()))
+    def spmm(row, pairs, unroll, src, flip):
+        axis = 0 if flip else 1
 
         def body(n, acc):
-            for u in range(UNROLL):
-                k = n * UNROLL + u
-                prod = lax.dot_general(tiles[lists[row, 2 * k]], src[lists[row + 1, 2 * k]], dims,
-                                       preferred_element_type=F32)
-                prod += lax.dot_general(tiles[lists[row, 2 * k + 1]], src[lists[row + 1, 2 * k + 1]], dims,
-                                        preferred_element_type=F32)
+            for u in range(unroll):
+                k = n * unroll + u
+                left = jnp.concatenate([tiles[lists[row, 2 * k]], tiles[lists[row, 2 * k + 1]]], axis=axis)
+                right = jnp.concatenate([src[lists[row + 1, 2 * k]], src[lists[row + 1, 2 * k + 1]]], axis=0)
+                prod = lax.dot_general(left, right, (((axis,), (0,)), ((), ())), preferred_element_type=F32)
                 acc = acc * lists[row + 2, k].astype(F32) + prod
                 runs[k] = acc.astype(BF16)
             return acc
 
-        lax.fori_loop(0, pairs // UNROLL, body, jnp.zeros((TILE, w), F32))
+        lax.fori_loop(0, pairs // unroll, body, jnp.zeros((TILE, w), F32))
 
     def collect(row, nd, dst):
         def body(r, _):
@@ -207,26 +215,35 @@
             pass
 
     ag = [gather(Row, xs[h], True) for h in range(H)]
-    for g in ag:
-        next(g)
+    next(ag[0])
 
     live_r = lax.broadcasted_iota(I32, (1, SLOTS), 1) < cnt[0, 0]
     live_c = lax.broadcasted_iota(I32, (SLOTS, 1), 0) < cnt[0, 0]
+    idx_c = jnp.transpose(idx_r[...])
     r_r, c_r = idx_r[0:1, :], idx_r[1:2, :]
     r_c, c_c = idx_c[:, 0:1], idx_c[:, 1:2]
     lists_v[...] = jnp.zeros_like(lists_v)
-    for row, (a, b, cc, nd, ns) in ((0, (r_r, r_c, c_c, NR, NC)), (4, (c_r, c_c, r_c, NC, NR))):
+
+    def put_lists(row, a, b, cc, nd, ns):
         t_l, s_l, k_l, e_l = pair_lists(a, b, cc, live_r, live_c, nd, ns)
         lists_v[row:row + 1, :] = t_l
         lists_v[row + 1:row + 2, :] = s_l
         lists_v[row + 2:row + 3, :] = k_l
         lists_v[row + 3:row + 4, 0:nd] = e_l
+
+    put_lists(0, r_r, r_c, c_c, NR, NC)
+    next(ag[0])
+    for g in ag[1:]:
+        next(g)
+    put_lists(4, c_r, c_c, r_c, NC, NR)
     cp = pltpu.make_async_copy(lists_v, lists, ls.at[1 + H * BLK])
     cp.start()
     runs[ZERO_RUN] = jnp.zeros((TILE, w), BF16)
     for h in range(H):
         xs[h][NC] = jnp.zeros((TILE, w), BF16)
         gs[h][NR] = jnp.zeros((TILE, w), BF16)
+    for g in ag[1:]:
+        next(g)
     cp.wait()
     load_tiles.wait()
 
@@ -238,14 +255,17 @@
     sc = []
     for h in range(H):
         finish(ag[h])
-        spmm(0, FPAIRS, xs[h], False)
+        spmm(0, FPAIRS, FUNROLL, xs[h], False)
         collect(0, NR, ps[h])
         g = scatter(Col, ps[h], 0, h, put_y(h))
         next(g)
         sc.append(g)
     for g in sc:
+        next(g)
+    for g in sc:
         finish(g)
 
+    load_grad.wait()
     wb = weight[...]
     bsum = jnp.zeros((1, 256), F32)
     for t in range(BLK):
@@ -260,33 +280,33 @@
         gw = lax.dot_general(pg, wb, (((1,), (1,)), ((), ())), preferred_element_type=F32).astype(BF16)
         for h in range(H):
             gs[h][j * BLK + t] = gw[:, h * w:(h + 1) * w]
+    stores = [pltpu.make_async_copy(output, output_hbm, ls.at[3 + H * BLK])]
+    stores[0].start()
     agc = [gather(Col, gs[h], False) for h in range(H)]
-    for g in agc:
-        next(g)
+    next(agc[0])
 
     dw = lax.dot_general(ybf[...], zb[...], (((0,), (0,)), ((), ())), preferred_element_type=F32)
     for k in range(8):
         dbuf[k, 0:32, :] = dw[k * 32:(k + 1) * 32, :]
         dbuf[k, 32:40, :] = jnp.broadcast_to(bsum, (8, 256))
+    drs[j] = dbuf[j]
+    next(agc[0])
+    for g in agc[1:]:
+        next(g)
+        next(g)
     s1 = [send(dbuf.at[lax.rem(j + d, 8)], drs.at[j], (i, lax.rem(j + d, 8))) for d in range(1, 8)]
-    drs[j] = dbuf[j]
-
-    for h in range(H):
-        next(agc[h])
-
-    for cp in s1:
-        cp.wait_recv()
-    tot = drs[0]
-    for k in range(1, 8):
-        tot = tot + drs[k]
     me4 = xl * 2 + c
-    dp[me4] = tot
-    s2 = []
-    for d in range(1, 4):
-        o = lax.rem(me4 + d, 4)
-        s2.append(send(dp.at[me4], dp.at[me4], (y * 4 + o, j)))
-
-    def grad_2():
+
+    def grad_1():
+        for cp in s1:
+            cp.wait_recv()
+        tot = drs[0]
+        for k in range(1, 8):
+            tot = tot + drs[k]
+        dp[me4] = tot
+        return [send(dp.at[me4], dp.at[me4], (y * 4 + lax.rem(me4 + d, 4), j)) for d in range(1, 4)]
+
+    def grad_2(s2):
         for cp in s2:
             cp.wait_recv()
         dq[y] = (dp[0] + dp[1]) + (dp[2] + dp[3])
@@ -298,42 +318,76 @@
         dfin[j] = (dq[0] + dq[1]) + (dq[2] + dq[3])
         return [send(dfin.at[j], dfin.at[j], (i, lax.rem(j + d, 8))) for d in range(1, 8)]
 
+    def grad_4(s4):
+        for cp in s4:
+            cp.wait_recv()
+        for k in range(8):
+            dw_out[k * 32:(k + 1) * 32, :] = dfin[k, 0:32, :]
+        db_out[...] = dfin[0, 32:33, :]
+        for a, b, n in ((dw_out, dw_hbm, 4), (db_out, db_hbm, 5)):
+            stores.append(pltpu.make_async_copy(a, b, ls.at[n + H * BLK]))
+            stores[-1].start()
+
     def put_f(h):
         def emit(t, v):
             fgrad[pl.ds(t * TILE, TILE), pl.ds(h * w, w)] = v.astype(BF16)
         return emit
 
-    late = None
-    back = []
-    for h in range(H):
-        finish(agc[h])
-        if h == 0:
-            s3 = grad_2()
-        spmm(4, BPAIRS, gs[h], True)
-        collect(4, NC, qs[h])
-        if h == 0:
-            s4 = grad_3(s3)
-        cps = {}
+    def to_sibling(h):
+        cps = []
         for k in range(8):
-            s = k * 2 + 1 - c
-            cps[k] = send(blk(qs[h], s), sib[h].at[pl.ds(k * BLK, BLK)], sibling)
+            cps.append(send(blk(qs[h], k * 2 + 1 - c), sib[h].at[pl.ds(k * BLK, BLK)], sibling))
+        return cps
+
+    def combine(h, cps):
         for k in range(8):
             cps[k].wait_recv()
             for t in range(BLK):
                 at = (k * 2 + c) * BLK + t
                 qs[h][at] = (qs[h][at].astype(F32) + sib[h][k * BLK + t].astype(F32)).astype(BF16)
+
+    back = []
+    finish(agc[0])
+    for h in range(H):
+        spmm(4, BPAIRS, BUNROLL, gs[h], True)
+        collect(4, NC, qs[h])
+        cps = to_sibling(h)
+        if h == 0:
+            s2 = grad_1()
+        else:
+            next(back[0])
+        if h == H - 1:
+            s3 = grad_2(s2)
+        else:
+            finish(agc[1])
+        combine(h, cps)
         g = scatter(Row, qs[h], 1, h, put_f(h))
         next(g)
         back.append(g)
-    for cp in s4:
-        cp.wait_recv()
-    for k in range(8):
-        dw_out[k * 32:(k + 1) * 32, :] = dfin[k, 0:32, :]
-    db_out[...] = dfin[0, 32:33, :]
+    s4 = grad_3(s3)
+    next(back[-1])
     for g in back:
         finish(g)
+    stores.append(pltpu.make_async_copy(fgrad, fgrad_hbm, ls.at[6 + H * BLK]))
+    stores[-1].start()
+    grad_4(s4)
+    for cp in stores:
+        cp.wait()
     for cp in sent:
         cp.wait_send()
+
+
+def tail(*refs):
+    src, dst, mid, sem = refs[:4], refs[4:8], refs[8:12], refs[12]
+    first = [pltpu.make_async_copy(src[n], mid[n], sem.at[n]) for n in range(4)]
+    second = [pltpu.make_async_copy(mid[n], dst[n], sem.at[4 + n]) for n in range(4)]
+    for cp in first:
+        cp.start()
+    for n in range(4):
+        first[n].wait()
+        second[n].start()
+    for cp in second:
+        cp.wait()
 
 
 def shards(H, features, weight, bias, tile_values, tile_index, tile_count, out_grad):
@@ -342,9 +396,11 @@
     many = lambda n, *s: [vm(n, *s)] * H
     blkT = (TILE, w)
     two = lambda n: [many(n, *blkT) for _ in range(2)]
-    index = tile_index[0, 0]
+    index_t = tile_index[0, 0].T
     sems = 180
     scratch = [
+        vm(512, 256), vm(512, 256), vm(512, 256),
+        vm(256, 256, dt=F32), vm(1, 256, dt=F32),
         vm(SLOTS, TILE, TILE),
         vm(ZERO_RUN + 1, *blkT),
         vm(8, 512, dt=I32),
@@ -358,30 +414,40 @@
         vm(512, 256), vm(512, 256),
         vm(8, 40, 256, dt=F32), vm(8, 40, 256, dt=F32), vm(4, 40, 256, dt=F32), vm(4, 40, 256, dt=F32),
         vm(8, 40, 256, dt=F32),
-        pltpu.SemaphoreType.DMA((sems,)), pltpu.SemaphoreType.DMA((sems,)), pltpu.SemaphoreType.DMA((2 + H * BLK,)),
+        pltpu.SemaphoreType.DMA((sems,)), pltpu.SemaphoreType.DMA((sems,)), pltpu.SemaphoreType.DMA((7 + H * BLK,)),
     ]
     vmem = pl.BlockSpec(memory_space=pltpu.VMEM)
-    out, fg, dw, db = pl.pallas_call(
+    hbm = pl.BlockSpec(memory_space=pl.ANY)
+    shapes = (
+        jax.ShapeDtypeStruct((512, 256), BF16),
+        jax.ShapeDtypeStruct((512, 256), BF16),
+        jax.ShapeDtypeStruct((256, 256), F32),
+        jax.ShapeDtypeStruct((1, 256), F32),
+    )
+    results = pl.pallas_call(
         functools.partial(kernel, H),
-        out_shape=(
-            jax.ShapeDtypeStruct((512, 256), BF16),
-            jax.ShapeDtypeStruct((512, 256), BF16),
-            jax.ShapeDtypeStruct((256, 256), F32),
-            jax.ShapeDtypeStruct((1, 256), F32),
-        ),
-        in_specs=[pl.BlockSpec(memory_space=pl.ANY), vmem, vmem, pl.BlockSpec(memory_space=pl.ANY), vmem, vmem,
-                  pl.BlockSpec(memory_space=pltpu.SMEM), vmem],
-        out_specs=(vmem,) * 4,
+        out_shape=shapes,
+        in_specs=[hbm, vmem, vmem, hbm, vmem, pl.BlockSpec(memory_space=pltpu.SMEM), hbm],
+        out_specs=(hbm,) * 4,
         scratch_shapes=scratch,
         compiler_params=pltpu.CompilerParams(collective_id=0, has_side_effects=True, vmem_limit_bytes=60 << 20),
         name="layer",
-    )(features, weight, bias.reshape(1, 256), tile_values, index, index.T, tile_count, out_grad)
+    )(features, weight, bias.reshape(1, 256), tile_values, index_t, tile_count, out_grad)
+    out, fg, dw, db = pl.pallas_call(
+        tail,
+        out_shape=shapes,
+        in_specs=[hbm] * 4,
+        out_specs=(hbm,) * 4,
+        scratch_shapes=[pltpu.VMEM(x.shape, x.dtype) for x in shapes] + [pltpu.SemaphoreType.DMA((8,))],
+        compiler_params=pltpu.CompilerParams(vmem_limit_bytes=60 << 20),
+        name="results",
+    )(*results)
     return out, fg, dw, db.reshape(256)
 
 
 def solution(mesh):
     return jax.shard_map(
-        functools.partial(shards, 1),
+        functools.partial(shards, 2),
         mesh=mesh,
         in_specs=(
             P(("row", "col"), None),

time: 155 us -> 110 us (0.71)
  Pallas kernels: 146 us -> 108 us
  local copies, waits for them, and re-layouts: 7.75 us -> 0 us
    pallas_call x1 -> x2, Pallas kernels: 146 us -> 108 us  [the longest x1 106 us: shards(): pl.pallas_call(functools.partial(kernel, H), out_shape=shapes, in_specs=[...]
    unnamed x4 -> x0, local copies, waits for them, and re-layouts: 6.23 us -> none
where the time goes in v2:
time: 110 us
  Pallas kernels  108 us (98%)
  between operations  1.29 us (1%)
    pallas_call x1, Pallas kernels, shards(): pl.pallas_call(functools.partial(kernel, H), out_shape=shapes, in_specs=[...  106 us

profile of v2, /device:TPU:1, one launch (start us, length us, event | category | flops | bytes accessed | tf_op | source)
XLA Modules:
  0.0 109.5 jit_solution(4304307531421071951)
XLA Ops:
  1.3 106.3 %layer.1 = (bf16[512,256]{1,0:T(8,128)(2,1)}, bf16[512,256]{1,0:T(8,128)(2,1)}, f32[256,256]{1,0:T(8,128)}, f32[1,256]{1,0:T(1,128)}) custom-call(bf16[512,256]{1,0:T(8,128)(2,1)} %feat.1, bf16[256,256]{1,0:T(8,128)(2,1)} %weight.1, f32[1,256]{1,0:T(1,128)} %bitcast.6, bf16[1,1,448,128,128]{4,3,2,1,0:T(8,128)(2,1)} %tiles_hbm.1, s32[2,448]{1,0:T(2,128)} %bitcast.5, ...), custom_call_target="tpu_custom_call" | custom-call | tf_op jit(solution)/shard_map/layer/pallas_call | solution.py:427
  107.6 1.9 %results.1 = (bf16[512,256]{1,0:T(8,128)(2,1)}, bf16[512,256]{1,0:T(8,128)(2,1)}, f32[256,256]{1,0:T(8,128)}, f32[1,256]{1,0:T(1,128)}) custom-call(bf16[512,256]{1,0:T(8,128)(2,1)} %get-tuple-element.12.refs_0_, bf16[512,256]{1,0:T(8,128)(2,1)} %get-tuple-element.13.refs_1_, f32[256,256]{1,0:T(8,128)} %get-tuple-element.14.refs_2_, ...), custom_call_target="tpu_custom_call" | custom-call | tf_op jit(solution)/shard_map/results/pallas_call | solution.py:436

commit v3 on v2

--- a/solution.py
+++ b/solution.py
@@ -14,7 +14,7 @@
 NR, NC = 32, 64
 FPAIRS, BPAIRS = 240, 256
 ZERO_RUN = 256
-FUNROLL, BUNROLL = 24, 32
+FUNROLL, BUNROLL = 48, 64
 F32, BF16, I32 = jnp.float32, jnp.bfloat16, jnp.int32
 
 
@@ -47,10 +47,10 @@
     return tile_l, src_l, keep_l, end_r
 
 
-def kernel(H, feat, weight, bias, tiles_hbm, idx_r, cnt, ograd_hbm,
+def kernel(H, feat, weight_hbm, bias_hbm, tiles_hbm, idx_hbm, cnt, ograd_hbm,
            output_hbm, fgrad_hbm, dw_hbm, db_hbm,
-           ograd, output, fgrad, dw_out, db_out, tiles, runs, lists_v, lists, xs, ps, gs, qs, sib, rsa, rsb, rsa2, rsb2, sa, sb, ybf, zb,
-           dbuf, drs, dp, dq, dfin, ss, rs, ls):
+           weight, bias, idx_r, ograd, output, fgrad, dw_out, db_out, tiles, runs, lists_v, lists, xs, ps, gs, qs, sib, rsa, rsb, rsa2, rsb2, sa, sb, ybf, zb,
+           dbuf, dsib, dsum, drs, dp, dfin, ss, rs, ls):
     w = 256 // H
     i, j = lax.axis_index("row"), lax.axis_index("col")
     y, xl, c = i // 4, lax.rem(i // 2, 2), lax.rem(i, 2)
@@ -91,8 +91,12 @@
             cp.start()
             loads.append(cp)
 
+    small = []
+    for n, (a, b) in enumerate(((idx_hbm, idx_r), (weight_hbm, weight), (bias_hbm, bias))):
+        small.append(pltpu.make_async_copy(a, b, ls.at[7 + H * BLK + n]))
+        small[-1].start()
+    load_grad.start()
     load_tiles.start()
-    load_grad.start()
     barrier = pltpu.get_barrier_semaphore()
     for r in peers:
         pl.semaphore_signal(barrier, inc=1, device_id=(r, j), device_id_type=MESH)
@@ -117,44 +121,65 @@
             part = blk(buf, s, lo, n)
             return send(part, part, dev)
 
-        me = g.slot(p, q)
-        first = {d: push(me, 0, 2, g.dev(m4(p + d), q)) for d in (1, 3, 2)}
-        cx = push(me, 0, BLK, g.dev(p, 1 - q))
+        me, other = g.slot(p, q), g.slot(p, 1 - q)
+        e = 1 - 2 * c
+        sides = (1, 3)
+        near = {d: g.slot(m4(p - d), q) for d in sides}
+        cross = g.dev(p, 1 - q)
+        ahead = g.dev(m4(p + e), q)
+        around = lambda s, lo: [push(s, lo, 2, g.dev(m4(p + d), q)) for d in sides]
+
+        def arrived(copies):
+            for cp in copies:
+                cp.wait_recv()
+
+        cx = push(me, 2, 2, cross)
+        f1 = around(me, 0)
+        cx2 = push(me, 0, 2, cross)
         pass_on(me, 0, BLK)
+        f2 = around(me, 2)
         yield
         cx.wait_recv()
-        other = g.slot(p, 1 - q)
-        second = {d: push(me, 2, 2, g.dev(m4(p + d), q)) for d in (1, 3, 2)}
-        third = {d: push(other, 2, 2, g.dev(m4(p + d), q)) for d in (1, 3, 2)}
+        f3 = around(other, 2)
+        arrived(f1)
+        w1 = push(g.slot(m4(p - e), q), 0, 2, ahead)
+        x1 = [push(near[d], 0, 2, cross) for d in sides]
+        yield
+        arrived(f2)
+        w2 = push(g.slot(m4(p - e), q), 2, 2, ahead)
+        for d in sides:
+            pass_on(near[d], 0, BLK)
+        cx2.wait_recv()
         pass_on(other, 0, BLK)
-        fourth = {}
-        for d in (1, 3, 2):
-            first[d].wait_recv()
-            fourth[d] = push(g.slot(m4(p - d), q), 0, 2, g.dev(p, 1 - q))
-        for d in (1, 3, 2):
-            pass_on(g.slot(m4(p - d), q), 0, 2)
+        w1.wait_recv()
+        x2 = push(g.slot(m4(p + 2), q), 0, 2, cross)
+        arrived(f3)
+        w3 = push(g.slot(m4(p - e), 1 - q), 2, 2, ahead)
         yield
-        for d in (1, 3, 2):
-            second[d].wait_recv()
-            pass_on(g.slot(m4(p - d), q), 2, 2)
-        for d in (1, 3, 2):
-            third[d].wait_recv()
-            fourth[d].wait_recv()
+        w2.wait_recv()
+        pass_on(g.slot(m4(p + 2), q), 0, BLK)
+        for u, d in zip(x1, sides):
+            u.wait_recv()
             pass_on(g.slot(m4(p - d), 1 - q), 0, BLK)
+        w3.wait_recv()
+        x2.wait_recv()
+        pass_on(g.slot(m4(p + 2), 1 - q), 0, BLK)
+        yield
         for cp in down:
             cp.wait_recv()
 
-    def scatter(g, buf, k, h, emit):
+    def scatter(g, buf, k, h, emit, ready):
         p, q = g.p, g.q
         ra, rb, ra2, rb2, oa, ob = rsa[k][h], rsb[k][h], rsa2[k][h], rsb2[k][h], sa[k][h], sb[k][h]
         xa, yb = {}, {}
         for d in (1, 3, 2, 0):
-            xa[d] = send(blk(buf, g.slot(m4(p + d), 1 - q), 0, 2), ra.at[pl.ds(2 * d, 2)], g.dev(p, 1 - q))
-        for d in (1, 3, 2):
-            for e in (1, 0):
-                qq = 1 - q if e else q
-                yb[d, e] = send(blk(buf, g.slot(m4(p + d), qq), 2, 2), rb.at[pl.ds((d - 1) * 4 + e * 2, 2)],
-                                g.dev(m4(p + d), q))
+            for f in (1, 0):
+                s = g.slot(m4(p + d), 1 - q if f else q)
+                ready(d, f, s)
+                if f:
+                    xa[d] = send(blk(buf, s, 0, 2), ra.at[pl.ds(2 * d, 2)], g.dev(p, 1 - q))
+                if d:
+                    yb[d, f] = send(blk(buf, s, 2, 2), rb.at[pl.ds((d - 1) * 4 + f * 2, 2)], g.dev(m4(p + d), q))
         yield
         y2 = {}
         for d in (1, 3, 2):
@@ -188,7 +213,7 @@
                 tot = tot + rb[(d - 1) * 4 + t].astype(F32)
             emit(2 + t, tot + rb2[t].astype(F32))
 
-    def spmm(row, pairs, unroll, src, flip):
+    def spmm(row, lo, hi, unroll, src, flip, acc=None):
         axis = 0 if flip else 1
 
         def body(n, acc):
@@ -201,14 +226,14 @@
                 runs[k] = acc.astype(BF16)
             return acc
 
-        lax.fori_loop(0, pairs // unroll, body, jnp.zeros((TILE, w), F32))
-
-    def collect(row, nd, dst):
-        def body(r, _):
-            dst[r] = runs[lists[row + 3, r]]
+        return lax.fori_loop(lo, hi, body, jnp.zeros((TILE, w), F32) if acc is None else acc)
+
+    def collect(row, slot, dst):
+        def body(t, _):
+            dst[slot * BLK + t] = runs[lists[row + 3, slot * BLK + t]]
             return 0
 
-        lax.fori_loop(0, nd, body, 0)
+        lax.fori_loop(0, BLK, body, 0)
 
     def finish(gen):
         for _ in gen:
@@ -217,8 +242,10 @@
     ag = [gather(Row, xs[h], True) for h in range(H)]
     next(ag[0])
 
-    live_r = lax.broadcasted_iota(I32, (1, SLOTS), 1) < cnt[0, 0]
-    live_c = lax.broadcasted_iota(I32, (SLOTS, 1), 0) < cnt[0, 0]
+    for cp in small:
+        cp.wait()
+    live_r = lax.broadcasted_iota(I32, (1, SLOTS), 1) < cnt[...]
+    live_c = lax.broadcasted_iota(I32, (SLOTS, 1), 0) < cnt[...]
     idx_c = jnp.transpose(idx_r[...])
     r_r, c_r = idx_r[0:1, :], idx_r[1:2, :]
     r_c, c_c = idx_c[:, 0:1], idx_c[:, 1:2]
@@ -232,6 +259,9 @@
         lists_v[row + 3:row + 4, 0:nd] = e_l
 
     put_lists(0, r_r, r_c, c_c, NR, NC)
+    next(ag[0])
+    for g in ag[1:]:
+        next(g)
     next(ag[0])
     for g in ag[1:]:
         next(g)
@@ -242,6 +272,7 @@
     for h in range(H):
         xs[h][NC] = jnp.zeros((TILE, w), BF16)
         gs[h][NR] = jnp.zeros((TILE, w), BF16)
+    next(ag[0])
     for g in ag[1:]:
         next(g)
     cp.wait()
@@ -255,9 +286,12 @@
     sc = []
     for h in range(H):
         finish(ag[h])
-        spmm(0, FPAIRS, FUNROLL, xs[h], False)
-        collect(0, NR, ps[h])
-        g = scatter(Col, ps[h], 0, h, put_y(h))
+        turns = FPAIRS // FUNROLL
+        acc = spmm(0, 0, turns - 1, FUNROLL, xs[h], False)
+        if h + 1 < H:
+            next(ag[h + 1])
+        spmm(0, turns - 1, turns, FUNROLL, xs[h], False, acc)
+        g = scatter(Col, ps[h], 0, h, put_y(h), lambda d, f, s: collect(0, s, ps[h]))
         next(g)
         sc.append(g)
     for g in sc:
@@ -286,44 +320,57 @@
     next(agc[0])
 
     dw = lax.dot_general(ybf[...], zb[...], (((0,), (0,)), ((), ())), preferred_element_type=F32)
-    for k in range(8):
-        dbuf[k, 0:32, :] = dw[k * 32:(k + 1) * 32, :]
-        dbuf[k, 32:40, :] = jnp.broadcast_to(bsum, (8, 256))
-    drs[j] = dbuf[j]
+    for k in range(16):
+        dbuf[k, 0:16, :] = dw[k * 16:(k + 1) * 16, :]
+        dbuf[k, 16:24, :] = jnp.broadcast_to(bsum, (8, 256))
+    s0 = send(dbuf.at[pl.ds((1 - c) * 8, 8)], dsib, sibling)
     next(agc[0])
     for g in agc[1:]:
         next(g)
-        next(g)
-    s1 = [send(dbuf.at[lax.rem(j + d, 8)], drs.at[j], (i, lax.rem(j + d, 8))) for d in range(1, 8)]
-    me4 = xl * 2 + c
-
-    def grad_1():
+    next(agc[0])
+    for g in agc[1:]:
+        next(g)
+    next(agc[0])
+    for g in agc[1:]:
+        next(g)
+    s0.wait_recv()
+    for k in range(8):
+        dsum[k] = dbuf[c * 8 + k] + dsib[k]
+    drs[j] = dsum[j]
+    chip = y * 2 + xl
+
+    def total(ref):
+        tot = ref[0]
+        for k in range(1, 8):
+            tot = tot + ref[k]
+        return tot
+
+    def grad_0():
+        return [send(dsum.at[lax.rem(j + d, 8)], drs.at[j], (i, lax.rem(j + d, 8))) for d in range(1, 8)]
+
+    def grad_1(s1):
         for cp in s1:
             cp.wait_recv()
-        tot = drs[0]
-        for k in range(1, 8):
-            tot = tot + drs[k]
-        dp[me4] = tot
-        return [send(dp.at[me4], dp.at[me4], (y * 4 + lax.rem(me4 + d, 4), j)) for d in range(1, 4)]
+        dp[chip] = total(drs)
+        return [send(dp.at[chip], dp.at[chip], (lax.rem(chip + d, 8) * 2 + c, j)) for d in range(1, 8)]
 
     def grad_2(s2):
         for cp in s2:
             cp.wait_recv()
-        dq[y] = (dp[0] + dp[1]) + (dp[2] + dp[3])
-        return [send(dq.at[y], dq.at[y], (m4(y + d) * 4 + me4, j)) for d in (1, 3, 2)]
+        dfin[c * 8 + j] = total(dp)
+        return [send(dfin.at[c * 8 + j], dfin.at[c * 8 + j], (i, lax.rem(j + d, 8))) for d in range(1, 8)]
 
     def grad_3(s3):
         for cp in s3:
             cp.wait_recv()
-        dfin[j] = (dq[0] + dq[1]) + (dq[2] + dq[3])
-        return [send(dfin.at[j], dfin.at[j], (i, lax.rem(j + d, 8))) for d in range(1, 8)]
+        half = dfin.at[pl.ds(c * 8, 8)]
+        return send(half, half, sibling)
 
     def grad_4(s4):
-        for cp in s4:
-            cp.wait_recv()
-        for k in range(8):
-            dw_out[k * 32:(k + 1) * 32, :] = dfin[k, 0:32, :]
-        db_out[...] = dfin[0, 32:33, :]
+        s4.wait_recv()
+        for k in range(16):
+            dw_out[k * 16:(k + 1) * 16, :] = dfin[k, 0:16, :]
+        db_out[...] = dfin[0, 16:17, :]
         for a, b, n in ((dw_out, dw_hbm, 4), (db_out, db_hbm, 5)):
             stores.append(pltpu.make_async_copy(a, b, ls.at[n + H * BLK]))
             stores[-1].start()
@@ -334,38 +381,52 @@
         return emit
 
     def to_sibling(h):
-        cps = []
-        for k in range(8):
-            cps.append(send(blk(qs[h], k * 2 + 1 - c), sib[h].at[pl.ds(k * BLK, BLK)], sibling))
+        cps = {}
+        chips = [(d, f, m4(y + d) * 2 + (1 - xl if f else xl)) for d in (1, 3, 2, 0) for f in (1, 0)]
+        for d, f, k in chips:
+            collect(4, k * 2 + 1 - c, qs[h])
+            cps[d, f] = send(blk(qs[h], k * 2 + 1 - c), sib[h].at[pl.ds(k * BLK, BLK)], sibling)
+        for d, f, k in chips:
+            collect(4, k * 2 + c, qs[h])
         return cps
 
-    def combine(h, cps):
-        for k in range(8):
-            cps[k].wait_recv()
-            for t in range(BLK):
-                at = (k * 2 + c) * BLK + t
-                qs[h][at] = (qs[h][at].astype(F32) + sib[h][k * BLK + t].astype(F32)).astype(BF16)
+    def combine(h, cp, s):
+        cp.wait_recv()
+
+        def body(t, _):
+            at = s * BLK + t
+            qs[h][at] = (qs[h][at].astype(F32) + sib[h][(s - c) * 2 + t].astype(F32)).astype(BF16)
+            return 0
+
+        lax.fori_loop(0, BLK, body, 0)
 
     back = []
     finish(agc[0])
+    def row_stage(h, cps):
+        g = scatter(Row, qs[h], 1, h, put_f(h), lambda d, f, s: combine(h, cps[d, f], s))
+        next(g)
+        back.append(g)
+
+    turns = BPAIRS // BUNROLL
     for h in range(H):
-        spmm(4, BPAIRS, BUNROLL, gs[h], True)
-        collect(4, NC, qs[h])
+        acc = spmm(4, 0, turns // 2, BUNROLL, gs[h], True)
+        if h > 0:
+            row_stage(0, cps)
+            s2 = grad_1(s1)
+        elif H == 1:
+            s1 = grad_0()
+        spmm(4, turns // 2, turns, BUNROLL, gs[h], True, acc)
         cps = to_sibling(h)
-        if h == 0:
-            s2 = grad_1()
-        else:
-            next(back[0])
-        if h == H - 1:
-            s3 = grad_2(s2)
-        else:
-            finish(agc[1])
-        combine(h, cps)
-        g = scatter(Row, qs[h], 1, h, put_f(h))
-        next(g)
-        back.append(g)
+        if h + 1 < H:
+            finish(agc[h + 1])
+            s1 = grad_0()
+    if H == 1:
+        s2 = grad_1(s1)
+    row_stage(H - 1, cps)
+    s3 = grad_2(s2)
+    for g in back:
+        next(g)
     s4 = grad_3(s3)
-    next(back[-1])
     for g in back:
         finish(g)
     stores.append(pltpu.make_async_copy(fgrad, fgrad_hbm, ls.at[6 + H * BLK]))
@@ -399,6 +460,7 @@
     index_t = tile_index[0, 0].T
     sems = 180
     scratch = [
+        vm(256, 256), vm(1, 256, dt=F32), vm(2, SLOTS, dt=I32),
         vm(512, 256), vm(512, 256), vm(512, 256),
         vm(256, 256, dt=F32), vm(1, 256, dt=F32),
         vm(SLOTS, TILE, TILE),
@@ -412,11 +474,10 @@
         many(32, *blkT),
         two(8), two(12), two(6), two(2), two(8), two(2),
         vm(512, 256), vm(512, 256),
-        vm(8, 40, 256, dt=F32), vm(8, 40, 256, dt=F32), vm(4, 40, 256, dt=F32), vm(4, 40, 256, dt=F32),
-        vm(8, 40, 256, dt=F32),
-        pltpu.SemaphoreType.DMA((sems,)), pltpu.SemaphoreType.DMA((sems,)), pltpu.SemaphoreType.DMA((7 + H * BLK,)),
+        vm(16, 24, 256, dt=F32), vm(8, 24, 256, dt=F32), vm(8, 24, 256, dt=F32), vm(8, 24, 256, dt=F32),
+        vm(8, 24, 256, dt=F32), vm(16, 24, 256, dt=F32),
+        pltpu.SemaphoreType.DMA((sems,)), pltpu.SemaphoreType.DMA((sems,)), pltpu.SemaphoreType.DMA((11 + H * BLK,)),
     ]
-    vmem = pl.BlockSpec(memory_space=pltpu.VMEM)
     hbm = pl.BlockSpec(memory_space=pl.ANY)
     shapes = (
         jax.ShapeDtypeStruct((512, 256), BF16),
@@ -427,7 +488,7 @@
     results = pl.pallas_call(
         functools.partial(kernel, H),
         out_shape=shapes,
-        in_specs=[hbm, vmem, vmem, hbm, vmem, pl.BlockSpec(memory_space=pltpu.SMEM), hbm],
+        in_specs=[hbm] * 5 + [pl.BlockSpec(memory_space=pltpu.VMEM), hbm],
         out_specs=(hbm,) * 4,
         scratch_shapes=scratch,
         compiler_params=pltpu.CompilerParams(collective_id=0, has_side_effects=True, vmem_limit_bytes=60 << 20),

time: 110 us -> 104 us (0.945)
  Pallas kernels: 108 us -> 102 us
    pallas_call x1, Pallas kernels: 106 us -> 100 us  [shards(): pl.pallas_call(functools.partial(kernel, H), out_shape=shapes, in_specs=[...]
where the time goes in v3:
time: 104 us
  Pallas kernels  102 us (98%)
  between operations  1.45 us (1%)
    pallas_call x1, Pallas kernels, shards(): pl.pallas_call(functools.partial(kernel, H), out_shape=shapes, in_specs=[...  100 us

profile of v3, /device:TPU:1, one launch (start us, length us, event | category | flops | bytes accessed | tf_op | source)
XLA Modules:
  0.0 103.7 jit_solution(17503914469365835637)
XLA Ops:
  1.3 100.4 %layer.1 = (bf16[512,256]{1,0:T(8,128)(2,1)}, bf16[512,256]{1,0:T(8,128)(2,1)}, f32[256,256]{1,0:T(8,128)}, f32[1,256]{1,0:T(1,128)}) custom-call(bf16[512,256]{1,0:T(8,128)(2,1)} %feat.1, bf16[256,256]{1,0:T(8,128)(2,1)} %weight_hbm.1, f32[1,256]{1,0:T(1,128)} %bitcast.6, bf16[1,1,448,128,128]{4,3,2,1,0:T(8,128)(2,1)} %tiles_hbm.1, s32[2,448]{1,0:T(2,128)} %bitcast.5, ...), custom_call_target="tpu_custom_call" | custom-call | tf_op jit(solution)/shard_map/layer/pallas_call | solution.py:488
  101.7 1.9 %results.1 = (bf16[512,256]{1,0:T(8,128)(2,1)}, bf16[512,256]{1,0:T(8,128)(2,1)}, f32[256,256]{1,0:T(8,128)}, f32[1,256]{1,0:T(1,128)}) custom-call(bf16[512,256]{1,0:T(8,128)(2,1)} %get-tuple-element.12.refs_0_, bf16[512,256]{1,0:T(8,128)(2,1)} %get-tuple-element.13.refs_1_, f32[256,256]{1,0:T(8,128)} %get-tuple-element.14.refs_2_, ...), custom_call_target="tpu_custom_call" | custom-call | tf_op jit(solution)/shard_map/results/pallas_call | solution.py:497

commit v4 on v3

--- a/solution.py
+++ b/solution.py
@@ -14,7 +14,7 @@
 NR, NC = 32, 64
 FPAIRS, BPAIRS = 240, 256
 ZERO_RUN = 256
-FUNROLL, BUNROLL = 48, 64
+FUNROLL, BUNROLL = 80, 128
 F32, BF16, I32 = jnp.float32, jnp.bfloat16, jnp.int32
 
 
@@ -71,7 +71,7 @@
     peers = [lax.rem(i + d, 16) for d in range(1, 16)]
     cpeers = [lax.rem(j + d, 8) for d in range(1, 8)]
 
-    sent = []
+    sent, drained = [], [0]
 
     def send(src, dst, dev):
         n = len(sent)
@@ -80,6 +80,11 @@
         cp.start()
         sent.append(cp)
         return cp
+
+    def drain(until):
+        for cp in sent[drained[0]:until]:
+            cp.wait_send()
+        drained[0] = until
 
     load_tiles = pltpu.make_async_copy(tiles_hbm.at[0, 0], tiles, ls.at[0])
     load_grad = pltpu.make_async_copy(ograd_hbm, ograd, ls.at[2 + H * BLK])
@@ -93,7 +98,7 @@
 
     small = []
     for n, (a, b) in enumerate(((idx_hbm, idx_r), (weight_hbm, weight), (bias_hbm, bias))):
-        small.append(pltpu.make_async_copy(a, b, ls.at[7 + H * BLK + n]))
+        small.append(pltpu.make_async_copy(a, b, ls.at[8 + H * BLK + n]))
         small[-1].start()
     load_grad.start()
     load_tiles.start()
@@ -422,20 +427,30 @@
             s1 = grad_0()
     if H == 1:
         s2 = grad_1(s1)
+    early = len(sent)
     row_stage(H - 1, cps)
     s3 = grad_2(s2)
-    for g in back:
-        next(g)
+    for g in back[:-1]:
+        next(g)
+    drain(early)
+    early = len(sent)
+    next(back[-1])
     s4 = grad_3(s3)
-    for g in back:
-        finish(g)
-    stores.append(pltpu.make_async_copy(fgrad, fgrad_hbm, ls.at[6 + H * BLK]))
+    for h in range(H - 1):
+        finish(back[h])
+        part = pl.ds(h * w, w)
+        stores.append(pltpu.make_async_copy(fgrad.at[:, part], fgrad_hbm.at[:, part], ls.at[6 + H * BLK]))
+        stores[-1].start()
+    drain(early)
+    early = len(sent)
+    grad_4(s4)
+    finish(back[-1])
+    part = pl.ds((H - 1) * w, w)
+    stores.append(pltpu.make_async_copy(fgrad.at[:, part], fgrad_hbm.at[:, part], ls.at[7 + H * BLK]))
     stores[-1].start()
-    grad_4(s4)
+    drain(len(sent))
     for cp in stores:
         cp.wait()
-    for cp in sent:
-        cp.wait_send()
 
 
 def tail(*refs):
@@ -476,7 +491,7 @@
         vm(512, 256), vm(512, 256),
         vm(16, 24, 256, dt=F32), vm(8, 24, 256, dt=F32), vm(8, 24, 256, dt=F32), vm(8, 24, 256, dt=F32),
         vm(8, 24, 256, dt=F32), vm(16, 24, 256, dt=F32),
-        pltpu.SemaphoreType.DMA((sems,)), pltpu.SemaphoreType.DMA((sems,)), pltpu.SemaphoreType.DMA((11 + H * BLK,)),
+        pltpu.SemaphoreType.DMA((sems,)), pltpu.SemaphoreType.DMA((sems,)), pltpu.SemaphoreType.DMA((12 + H * BLK,)),
     ]
     hbm = pl.BlockSpec(memory_space=pl.ANY)
     shapes = (

time: 104 us -> 101 us (0.971)
  Pallas kernels: 102 us -> 99.2 us
    pallas_call x1, Pallas kernels: 100 us -> 97.3 us  [shards(): pl.pallas_call(functools.partial(kernel, H), out_shape=shapes, in_specs=[...]
where the time goes in v4:
time: 101 us
  Pallas kernels  99.2 us (98%)
  between operations  1.45 us (1%)
    pallas_call x1, Pallas kernels, shards(): pl.pallas_call(functools.partial(kernel, H), out_shape=shapes, in_specs=[...  97.3 us

profile of v4, /device:TPU:1, one launch (start us, length us, event | category | flops | bytes accessed | tf_op | source)
XLA Modules:
  0.0 100.6 jit_solution(7492919899631108799)
XLA Ops:
  1.3 97.3 %layer.1 = (bf16[512,256]{1,0:T(8,128)(2,1)}, bf16[512,256]{1,0:T(8,128)(2,1)}, f32[256,256]{1,0:T(8,128)}, f32[1,256]{1,0:T(1,128)}) custom-call(bf16[512,256]{1,0:T(8,128)(2,1)} %feat.1, bf16[256,256]{1,0:T(8,128)(2,1)} %weight_hbm.1, f32[1,256]{1,0:T(1,128)} %bitcast.6, bf16[1,1,448,128,128]{4,3,2,1,0:T(8,128)(2,1)} %tiles_hbm.1, s32[2,448]{1,0:T(2,128)} %bitcast.5, ...), custom_call_target="tpu_custom_call" | custom-call | tf_op jit(solution)/shard_map/layer/pallas_call | solution.py:503
  98.5 1.9 %results.1 = (bf16[512,256]{1,0:T(8,128)(2,1)}, bf16[512,256]{1,0:T(8,128)(2,1)}, f32[256,256]{1,0:T(8,128)}, f32[1,256]{1,0:T(1,128)}) custom-call(bf16[512,256]{1,0:T(8,128)(2,1)} %get-tuple-element.12.refs_0_, bf16[512,256]{1,0:T(8,128)(2,1)} %get-tuple-element.13.refs_1_, f32[256,256]{1,0:T(8,128)} %get-tuple-element.14.refs_2_, ...), custom_call_target="tpu_custom_call" | custom-call | tf_op jit(solution)/shard_map/results/pallas_call | solution.py:512

commit v5 on v4

--- a/solution.py
+++ b/solution.py
@@ -68,7 +68,7 @@
         dev = staticmethod(lambda p, q: (i, q * 4 + p))
 
     sibling = ((y * 2 + xl) * 2 + 1 - c, j)
-    peers = [lax.rem(i + d, 16) for d in range(1, 16)]
+    peers = [lax.rem(y * 2 + xl + d, 8) * 2 + c for d in range(1, 8)] + [(y * 2 + xl) * 2 + 1 - c]
     cpeers = [lax.rem(j + d, 8) for d in range(1, 8)]
 
     sent, drained = [], [0]
@@ -107,7 +107,7 @@
         pl.semaphore_signal(barrier, inc=1, device_id=(r, j), device_id_type=MESH)
     for k in cpeers:
         pl.semaphore_signal(barrier, inc=1, device_id=(i, k), device_id_type=MESH)
-    pl.semaphore_wait(barrier, 22)
+    pl.semaphore_wait(barrier, 15)
     for cp in loads:
         cp.wait()
 

time: 101 us -> 101 us (level)
  no operation moved by 1% of the time
where the time goes in v5:
time: 101 us
  Pallas kernels  99.1 us (98%)
  between operations  1.45 us (1%)
    pallas_call x1, Pallas kernels, shards(): pl.pallas_call(functools.partial(kernel, H), out_shape=shapes, in_specs=[...  97.2 us

profile of v5, /device:TPU:1, one launch (start us, length us, event | category | flops | bytes accessed | tf_op | source)
XLA Modules:
  0.0 100.6 jit_solution(13756146183919867146)
XLA Ops:
  1.3 97.2 %layer.1 = (bf16[512,256]{1,0:T(8,128)(2,1)}, bf16[512,256]{1,0:T(8,128)(2,1)}, f32[256,256]{1,0:T(8,128)}, f32[1,256]{1,0:T(1,128)}) custom-call(bf16[512,256]{1,0:T(8,128)(2,1)} %feat.1, bf16[256,256]{1,0:T(8,128)(2,1)} %weight_hbm.1, f32[1,256]{1,0:T(1,128)} %bitcast.6, bf16[1,1,448,128,128]{4,3,2,1,0:T(8,128)(2,1)} %tiles_hbm.1, s32[2,448]{1,0:T(2,128)} %bitcast.5, ...), custom_call_target="tpu_custom_call" | custom-call | tf_op jit(solution)/shard_map/layer/pallas_call | solution.py:503
  98.5 1.9 %results.1 = (bf16[512,256]{1,0:T(8,128)(2,1)}, bf16[512,256]{1,0:T(8,128)(2,1)}, f32[256,256]{1,0:T(8,128)}, f32[1,256]{1,0:T(1,128)}) custom-call(bf16[512,256]{1,0:T(8,128)(2,1)} %get-tuple-element.12.refs_0_, bf16[512,256]{1,0:T(8,128)(2,1)} %get-tuple-element.13.refs_1_, f32[256,256]{1,0:T(8,128)} %get-tuple-element.14.refs_2_, ...), custom_call_target="tpu_custom_call" | custom-call | tf_op jit(solution)/shard_map/results/pallas_call | solution.py:512
